TPU v7x, 32 devices: a whole 2x2x4 slice. The times are simulated.
32 devices in a mesh: dp: 8 (over z, x), tensor: 4 (over y, core).
Axes of the slice: x: 2, y: 2, z: 4, core: 2. Of those that a mesh axis runs over, the one named last changes fastest.
Arguments:
- hidden_in: bfloat16 [16384, 640], P('dp'), may hold values from -6 to 6
- query_weight: bfloat16 [640, 1024], P(None, 'tensor'), may hold values from -0.25 to 0.25
- key_weight: bfloat16 [640, 256], replicated, may hold values from -0.25 to 0.25
- value_weight: bfloat16 [640, 256], replicated, may hold values from -0.25 to 0.25
- output_weight: bfloat16 [1024, 640], P('tensor'), may hold values from -0.1875 to 0.1875
- gate_weight: bfloat16 [640, 2048], P(None, 'tensor'), may hold values from -0.25 to 0.25
- up_weight: bfloat16 [640, 2048], P(None, 'tensor'), may hold values from -0.25 to 0.25
- down_weight: bfloat16 [2048, 640], P('tensor'), may hold values from -0.125 to 0.125
- pre_attention: float32 [640], replicated, may hold values from -0.5 to 0.5
- query_norm: float32 [256], replicated, may hold values from -0.5 to 0.5
- key_norm: float32 [256], replicated, may hold values from -0.5 to 0.5
- post_attention: float32 [640], replicated, may hold values from -0.5 to 0.5
- pre_feedforward: float32 [640], replicated, may hold values from -0.5 to 0.5
- post_feedforward: float32 [640], replicated, may hold values from -0.5 to 0.5
- segments: int32 [16384], P('dp'), may hold values from 0 to 15, as said below
- positions: int32 [16384], P('dp'), may hold values from 0 to 511, as said below
- cotangent: bfloat16 [16384, 640], P('dp'), may hold values from -6 to 6
Outputs:
- hidden_out: bfloat16 [16384, 640], P('dp')
- grad_input: float32 [16384, 640], P('dp')
- grad_query_weight: float32 [640, 1024], P(None, 'tensor')
- grad_key_weight: float32 [640, 256], replicated
- grad_value_weight: float32 [640, 256], replicated
- grad_output_weight: float32 [1024, 640], P('tensor')
- grad_gate_weight: float32 [640, 2048], P(None, 'tensor')
- grad_up_weight: float32 [640, 2048], P(None, 'tensor')
- grad_down_weight: float32 [2048, 640], P('tensor')
- grad_pre_attention: float32 [640], replicated
- grad_query_norm: float32 [256], replicated
- grad_key_norm: float32 [256], replicated
- grad_post_attention: float32 [640], replicated
- grad_pre_feedforward: float32 [640], replicated
- grad_post_feedforward: float32 [640], replicated
Inputs may be any that keep to these rules, and one draw needn't show every extreme that they name: `segments`: within each aligned block of 512 tokens the document numbers start at 0 at the block's first token and rise by 0 or 1 from one token to the next. `positions`: each token's position is its distance from the first token of its document in the same block.
All inputs are finite; a program needn't handle non-finite values.
Results may differ from a plain program's by a relative error of at most 0.02.
Values may be sent and summed in bfloat16 or wider, within the bound.
A program may use at most 128 MiB of HBM per device.

v0:
```python
import jax
import jax.numpy as jnp
from jax import lax
from jax.sharding import PartitionSpec as P

LEN = 512
epsilon = 1e-06
rope_base = 1000000.0
masked_score = -1e30


def normed(values, norm_gain):
    inverse = lax.rsqrt(jnp.mean(values * values, axis=-1, keepdims=True) + epsilon)
    return values * inverse * (1.0 + norm_gain)


def rotary(values, cosine, sine_table):
    half_width = values.shape[-1] // 2
    front_half = values[..., :half_width]
    second = values[..., half_width:]
    return jnp.concatenate(
        [front_half * cosine - second * sine_table, second * cosine + front_half * sine_table],
        axis=-1,
    )


def rotary_tables(positions, head_width):
    steps_half = jnp.arange(head_width // 2).astype(jnp.float32)
    frequency = jnp.power(jnp.float32(rope_base), -2.0 * steps_half / head_width)
    angles = positions.astype(jnp.float32)[:, None] * frequency[None, :]
    return (jnp.cos(angles), jnp.sin(angles))


def gated(gate_proj, up_proj):
    return jax.nn.gelu(gate_proj, approximate=True) * up_proj


def pack_mask(segment):
    offsets = jnp.arange(segment.shape[0])
    return (segment[:, None] == segment[None, :]) & (offsets[None, :] <= offsets[:, None])


def pack_scores(queries, key_rows, segment):
    score_scale = queries.shape[-1] ** (-0.5)
    scores = (
        jnp.einsum("ihd,jd->hij", queries, key_rows, preferred_element_type=jnp.float32)
        * score_scale
    )
    return jnp.where(pack_mask(segment)[None], scores, masked_score)


def attend_pack(inputs):
    queries, key_rows, values, segment = inputs
    scores = pack_scores(queries, key_rows, segment)
    top_score = jnp.max(scores, axis=-1, keepdims=True)
    log_total = top_score + jnp.log(jnp.sum(jnp.exp(scores - top_score), axis=-1, keepdims=True))
    prob_low = jnp.exp(scores - log_total).astype(jnp.bfloat16)
    mixture = jnp.einsum("hij,jd->ihd", prob_low, values, preferred_element_type=jnp.float32)
    return (mixture.astype(jnp.bfloat16), log_total)


def attend_back(inputs):
    queries, key_rows, values, segment, log_total, mixture_grad = inputs
    score_scale = queries.shape[-1] ** (-0.5)
    probability = jnp.exp(pack_scores(queries, key_rows, segment) - log_total)
    prob_low = probability.astype(jnp.bfloat16)
    value_grad = jnp.einsum(
        "hij,ihd->jhd", prob_low, mixture_grad, preferred_element_type=jnp.float32
    )
    prob_grad = jnp.einsum("ihd,jd->hij", mixture_grad, values, preferred_element_type=jnp.float32)
    row_terms = jnp.sum(probability * prob_grad, axis=-1, keepdims=True)
    score_grad = (probability * (prob_grad - row_terms)).astype(jnp.bfloat16)
    query_grad = (
        jnp.einsum("hij,jd->ihd", score_grad, key_rows, preferred_element_type=jnp.float32)
        * score_scale
    )
    key_grad = (
        jnp.einsum("hij,ihd->jhd", score_grad, queries, preferred_element_type=jnp.float32)
        * score_scale
    )
    return (query_grad, key_grad, value_grad.astype(jnp.bfloat16))


def run_layer(
    hidden_in,
    query_weight,
    key_weight,
    value_weight,
    output_weight,
    gate_weight,
    up_weight,
    down_weight,
    pre_attention,
    query_norm,
    key_norm,
    post_attention,
    pre_feedforward,
    post_feedforward,
    segments,
    positions,
    cotangent,
    reducers,
    feed_hook,
):
    attention_reduce, feed_reduce, feed_back_reduce, attention_back_reduce = reducers
    tokens = hidden_in.shape[0]
    pack_length = LEN
    pack_count = tokens // pack_length
    head_width = key_weight.shape[1]
    local_heads = query_weight.shape[1] // head_width
    hidden = hidden_in.astype(jnp.float32)
    cosine, sine_table = rotary_tables(positions, head_width)

    def head_path(projected, norm_gain):
        return rotary(normed(projected, norm_gain), cosine[:, None, :], sine_table[:, None, :])

    normed_value, pre_back = jax.vjp(normed, hidden, pre_attention)
    normed_in = normed_value.astype(jnp.bfloat16)
    query_proj = jnp.dot(normed_in, query_weight, preferred_element_type=jnp.float32)
    query_proj = query_proj.reshape(tokens, local_heads, head_width)
    key_proj = jnp.dot(normed_in, key_weight, preferred_element_type=jnp.float32)
    value_low = jnp.dot(normed_in, value_weight, preferred_element_type=jnp.float32).astype(
        jnp.bfloat16
    )
    query_rot, query_back = jax.vjp(head_path, query_proj, query_norm)
    key_heads = key_proj[:, None, :]
    key_rot, key_back = jax.vjp(head_path, key_heads, key_norm)
    query_packs = query_rot.astype(jnp.bfloat16).reshape(
        pack_count, pack_length, local_heads, head_width
    )
    key_packs = key_rot[:, 0, :].astype(jnp.bfloat16).reshape(pack_count, pack_length, head_width)
    value_packs = value_low.reshape(pack_count, pack_length, head_width)
    segment_packs = segments.reshape(pack_count, pack_length)
    mixture, log_total = lax.map(attend_pack, (query_packs, key_packs, value_packs, segment_packs))
    mixture_low = mixture.reshape(tokens, local_heads * head_width)
    attention = attention_reduce(
        jnp.dot(mixture_low, output_weight, preferred_element_type=jnp.float32)
    )
    post_value, post_att_back = jax.vjp(normed, attention, post_attention)
    middle = hidden + post_value
    mid_value, mid_back = jax.vjp(normed, middle, pre_feedforward)
    normed_mid = mid_value.astype(jnp.bfloat16)
    gate_proj = jnp.dot(normed_mid, gate_weight, preferred_element_type=jnp.float32)
    up_proj = jnp.dot(normed_mid, up_weight, preferred_element_type=jnp.float32)
    product, gated_back = jax.vjp(gated, gate_proj, up_proj)
    product_low = product.astype(jnp.bfloat16)
    feed = feed_reduce(jnp.dot(product_low, down_weight, preferred_element_type=jnp.float32))
    feed_value, feed_out_back = jax.vjp(normed, feed, post_feedforward)
    hidden_out = (middle + feed_value).astype(jnp.bfloat16)
    cotangent_full = cotangent.astype(jnp.float32)
    feed_grad, grad_post_feedforward = feed_out_back(cotangent_full)
    feed_grad_low = feed_grad.astype(jnp.bfloat16)
    grad_down_weight = jnp.einsum(
        "tf,td->fd", product_low, feed_grad_low, preferred_element_type=jnp.float32
    )
    product_grad = jnp.einsum(
        "td,fd->tf", feed_grad_low, down_weight, preferred_element_type=jnp.float32
    )
    gate_grad, up_grad = gated_back(product_grad)
    gate_grad_low = gate_grad.astype(jnp.bfloat16)
    up_grad_low = up_grad.astype(jnp.bfloat16)
    grad_gate_weight = jnp.einsum(
        "td,tf->df", normed_mid, gate_grad_low, preferred_element_type=jnp.float32
    )
    grad_up_weight = jnp.einsum(
        "td,tf->df", normed_mid, up_grad_low, preferred_element_type=jnp.float32
    )
    grad_gate_weight, grad_up_weight, grad_down_weight, grad_post_feedforward = feed_hook(
        (grad_gate_weight, grad_up_weight, grad_down_weight, grad_post_feedforward)
    )
    mid_part = jnp.einsum(
        "tf,df->td", gate_grad_low, gate_weight, preferred_element_type=jnp.float32
    )
    mid_part = mid_part + jnp.einsum(
        "tf,df->td", up_grad_low, up_weight, preferred_element_type=jnp.float32
    )
    mid_normed_grad = feed_back_reduce(mid_part)
    middle_part, grad_pre_feedforward = mid_back(mid_normed_grad)
    middle_grad = cotangent_full + middle_part
    attention_grad, grad_post_attention = post_att_back(middle_grad)
    attention_grad_low = attention_grad.astype(jnp.bfloat16)
    grad_output_weight = jnp.einsum(
        "tk,td->kd", mixture_low, attention_grad_low, preferred_element_type=jnp.float32
    )
    mixture_grad = jnp.einsum(
        "td,kd->tk", attention_grad_low, output_weight, preferred_element_type=jnp.float32
    )
    mixture_grad_packs = mixture_grad.astype(jnp.bfloat16).reshape(
        pack_count, pack_length, local_heads, head_width
    )
    query_rot_grad, key_rot_grad, value_grad_low = lax.map(
        attend_back,
        (query_packs, key_packs, value_packs, segment_packs, log_total, mixture_grad_packs),
    )
    query_grad, grad_query_norm = query_back(
        query_rot_grad.reshape(tokens, local_heads, head_width)
    )
    key_grad, grad_key_norm = key_back(key_rot_grad.reshape(tokens, local_heads, head_width))
    query_grad_low = query_grad.astype(jnp.bfloat16).reshape(tokens, local_heads * head_width)
    key_grad_low = key_grad.astype(jnp.bfloat16)
    value_grad_low = value_grad_low.reshape(tokens, local_heads, head_width)
    grad_query_weight = jnp.einsum(
        "td,tk->dk", normed_in, query_grad_low, preferred_element_type=jnp.float32
    )
    grad_key_weight = jnp.einsum(
        "td,thk->dk", normed_in, key_grad_low, preferred_element_type=jnp.float32
    )
    grad_value_weight = jnp.einsum(
        "td,thk->dk", normed_in, value_grad_low, preferred_element_type=jnp.float32
    )
    in_part = jnp.einsum(
        "tk,dk->td", query_grad_low, query_weight, preferred_element_type=jnp.float32
    )
    in_part = in_part + jnp.einsum(
        "thk,dk->td", key_grad_low, key_weight, preferred_element_type=jnp.float32
    )
    in_part = in_part + jnp.einsum(
        "thk,dk->td", value_grad_low, value_weight, preferred_element_type=jnp.float32
    )
    in_normed_grad = attention_back_reduce(in_part)
    input_part, grad_pre_attention = pre_back(in_normed_grad)
    grad_input = middle_grad + input_part
    return (
        hidden_out,
        grad_input,
        grad_query_weight,
        grad_key_weight,
        grad_value_weight,
        grad_output_weight,
        grad_gate_weight,
        grad_up_weight,
        grad_down_weight,
        grad_pre_attention,
        grad_query_norm,
        grad_key_norm,
        grad_post_attention,
        grad_pre_feedforward,
        grad_post_feedforward,
    )


def on_device(
    hidden_in,
    query_weight,
    key_weight,
    value_weight,
    output_weight,
    gate_weight,
    up_weight,
    down_weight,
    pre_attention,
    query_norm,
    key_norm,
    post_attention,
    pre_feedforward,
    post_feedforward,
    segments,
    positions,
    cotangent,
):

    def attention_reduce(values):
        return lax.psum(values, "tensor")

    def feed_reduce(values):
        return lax.psum(values.astype(jnp.bfloat16), "tensor").astype(jnp.float32)

    def feed_back_reduce(values):
        return lax.psum(values.astype(jnp.bfloat16), "tensor").astype(jnp.float32)

    def attention_back_reduce(values):
        return lax.psum(values.astype(jnp.bfloat16), "tensor").astype(jnp.float32)

    def feed_hook(grads):
        return grads

    (
        hidden_out,
        grad_input,
        grad_query_weight,
        grad_key_weight,
        grad_value_weight,
        grad_output_weight,
        grad_gate_weight,
        grad_up_weight,
        grad_down_weight,
        grad_pre_attention,
        grad_query_norm,
        grad_key_norm,
        grad_post_attention,
        grad_pre_feedforward,
        grad_post_feedforward,
    ) = run_layer(
        hidden_in,
        query_weight,
        key_weight,
        value_weight,
        output_weight,
        gate_weight,
        up_weight,
        down_weight,
        pre_attention,
        query_norm,
        key_norm,
        post_attention,
        pre_feedforward,
        post_feedforward,
        segments,
        positions,
        cotangent,
        (attention_reduce, feed_reduce, feed_back_reduce, attention_back_reduce),
        feed_hook,
    )
    grad_key_weight, grad_value_weight, grad_query_norm, grad_key_norm = lax.psum(
        (grad_key_weight, grad_value_weight, grad_query_norm, grad_key_norm), ("dp", "tensor")
    )
    (
        grad_query_weight,
        grad_output_weight,
        grad_gate_weight,
        grad_up_weight,
        grad_down_weight,
        grad_pre_attention,
        grad_post_attention,
        grad_pre_feedforward,
        grad_post_feedforward,
    ) = lax.psum(
        (
            grad_query_weight,
            grad_output_weight,
            grad_gate_weight,
            grad_up_weight,
            grad_down_weight,
            grad_pre_attention,
            grad_post_attention,
            grad_pre_feedforward,
            grad_post_feedforward,
        ),
        "dp",
    )
    return (
        hidden_out,
        grad_input,
        grad_query_weight,
        grad_key_weight,
        grad_value_weight,
        grad_output_weight,
        grad_gate_weight,
        grad_up_weight,
        grad_down_weight,
        grad_pre_attention,
        grad_query_norm,
        grad_key_norm,
        grad_post_attention,
        grad_pre_feedforward,
        grad_post_feedforward,
    )


def solution(mesh):
    placed = (
        P("dp", None),
        P(None, "tensor"),
        P(),
        P(),
        P("tensor", None),
        P(None, "tensor"),
        P(None, "tensor"),
        P("tensor", None),
        P(),
        P(),
        P(),
        P(),
        P(),
        P(),
        P("dp"),
        P("dp"),
        P("dp", None),
    )
    return jax.shard_map(
        on_device,
        mesh=mesh,
        in_specs=placed,
        out_specs=(
            P("dp", None),
            P("dp", None),
            P(None, "tensor"),
            P(),
            P(),
            P("tensor", None),
            P(None, "tensor"),
            P(None, "tensor"),
            P("tensor", None),
            P(),
            P(),
            P(),
            P(),
            P(),
            P(),
        ),
        check_vma=False,
    )
```

profile of v0, /device:TPU:0, one launch (start us, length us, event | category | flops | bytes accessed | tf_op | source)
XLA Modules:
  0.0 909.8 jit_solution(12823472843531258651)
XLA Ops:
  7.3 2.5 fusion.63
  10.8 2.4 multiply_reduce_fusion.6
  13.2 2.3 multiply_reduce_fusion.5
  15.6 3.0 copy.42
  18.6 2.6 multiply_bitcast_fusion
  21.3 5.7 fusion.99
  31.1 2.3 pad_maximum_fusion
  33.4 2.3 copy.56
  35.6 3.7 convolution_convert_fusion.4
  40.0 2.3 pad_maximum_fusion.1
  43.3 26.9 %while.26 = (s32[]{:T(128)}, bf16[4,512,1,256]{3,1,0,2:T(8,128)(2,1)}, f32[4,1,512,1]{2,3,1,0:T(1,128)}, bf16[4,512,256]{2,1,0:T(8,128)(2,1)}, s32[4,512]{1,0:T(...) while((s32[]{:T(128)}, bf16[4,512,1,256]{3,1,0,2:T(8,128)(2,1)}, ...), condition=%wide.region_6.7_spmd, body=%wide.region_3.6_spmd.sunk | while | flops 271187456 | bytes 5272153 | solution.py:134
  70.2 4.6 fusion.115
  75.6 104.7 %all-reduce.15.cloned.1.call-done = f32[2048,640]{1,0:T(8,128)} async-done(((f32[2048,640]{1,0:T(8,128)}), f32[2048,640]{1,0:T(8,128)}) %all-reduce.15.cloned.1.call-update) | async-done | bytes 5242896 | tf_op jit(solution)/shard_map/psum | solution.py:263
  180.3 3.0 multiply_reduce_fusion.4
  190.1 4.1 multiply_convert_fusion.3
  195.5 3.3 convolution_convert_fusion.2
  199.4 59.6 %all-reduce.17.cloned.1.call-done = bf16[2048,640]{1,0:T(8,128)(2,1)} async-done(((bf16[2048,640]{1,0:T(8,128)(2,1)}), bf16[2048,640]{1,0:T(8,128)(2,1)}) %all-reduce.17.cloned.1.call-update) | async-done | bytes 2621456 | tf_op jit(solution)/shard_map/psum | solution.py:266
  259.0 2.5 fusion.61
  261.5 4.2 fusion.57
  267.9 4.9 multiply_convert_fusion.2
  274.8 3.3 add_convert_fusion.1
  278.4 5.3 fusion.126
  283.6 54.6 %all-reduce.19.cloned.1.call-done = bf16[2048,640]{1,0:T(8,128)(2,1)} async-done(((bf16[2048,640]{1,0:T(8,128)(2,1)}), bf16[2048,640]{1,0:T(8,128)(2,1)}) %all-reduce.19.cloned.1.call-update) | async-done | bytes 2621456 | tf_op jit(solution)/shard_map/psum | solution.py:269
  338.3 4.4 fusion.55
  343.1 7.7 multiply_reduce_fusion.1
  355.8 125.7 %while.27 = (s32[]{:T(128)}, f32[4,512,1,256]{1,0,3,2:T(4,128)}, f32[4,512,1,256]{1,0,3,2:T(4,128)}, bf16[4,512,1,256]{3,1,0,2:T(8,128)(2,1)}, bf16[4,512,256]{2...) while((s32[]{:T(128)}, f32[4,512,1,256]{1,0,3,2:T(4,128)}, ...), condition=%wide.region_18.19_spmd, body=%wide.region_16.18_spmd.sunk | while | flops 674627072 | bytes 16275081 | solution.py:191
  362.1 11.0 %dynamic_update_slice.30 = f32[4,512,1,256]{1,0,3,2:T(4,128)} dynamic-update-slice(f32[4,512,1,256]{1,0,3,2:T(4,128)} %get-tuple-element.387, f32[1,512,1,256]{1,0,3,2:T(1,128)S(1)} %copy.93, s32[]{:T(128)} %get-tuple-element.385, s32[]{:T(128)} %constant.83.clone.1..sunk, s32[]{:T(128)} %constant.83.clone.1..sunk, s32[]{:T(128)} %constant.83.clone.1..sunk) | dynamic-update-slice | bytes 1048580 | tf_op jit(solution)/shard_map/while/body/jit(dynamic_update_index_in_dim)/dynamic_update_slice | solution.py:191
  374.9 11.1 %dynamic_update_slice.29 = f32[4,512,1,256]{1,0,3,2:T(4,128)} dynamic-update-slice(f32[4,512,1,256]{1,0,3,2:T(4,128)} %get-tuple-element.386, f32[1,512,1,256]{1,0,3,2:T(1,128)S(1)} %copy.92, s32[]{:T(128)} %get-tuple-element.385, s32[]{:T(128)} %constant.83.clone.1..sunk, s32[]{:T(128)} %constant.83.clone.1..sunk, s32[]{:T(128)} %constant.83.clone.1..sunk) | dynamic-update-slice | bytes 1048580 | tf_op jit(solution)/shard_map/while/body/jit(dynamic_update_index_in_dim)/dynamic_update_slice | solution.py:191
  393.5 11.0 %dynamic_update_slice.30 = f32[4,512,1,256]{1,0,3,2:T(4,128)} dynamic-update-slice(f32[4,512,1,256]{1,0,3,2:T(4,128)} %get-tuple-element.387, f32[1,512,1,256]{1,0,3,2:T(1,128)S(1)} %copy.93, s32[]{:T(128)} %get-tuple-element.385, s32[]{:T(128)} %constant.83.clone.1..sunk, s32[]{:T(128)} %constant.83.clone.1..sunk, s32[]{:T(128)} %constant.83.clone.1..sunk) | dynamic-update-slice | bytes 1048580 | tf_op jit(solution)/shard_map/while/body/jit(dynamic_update_index_in_dim)/dynamic_update_slice | solution.py:191
  406.3 11.1 %dynamic_update_slice.29 = f32[4,512,1,256]{1,0,3,2:T(4,128)} dynamic-update-slice(f32[4,512,1,256]{1,0,3,2:T(4,128)} %get-tuple-element.386, f32[1,512,1,256]{1,0,3,2:T(1,128)S(1)} %copy.92, s32[]{:T(128)} %get-tuple-element.385, s32[]{:T(128)} %constant.83.clone.1..sunk, s32[]{:T(128)} %constant.83.clone.1..sunk, s32[]{:T(128)} %constant.83.clone.1..sunk) | dynamic-update-slice | bytes 1048580 | tf_op jit(solution)/shard_map/while/body/jit(dynamic_update_index_in_dim)/dynamic_update_slice | solution.py:191
  425.0 11.0 %dynamic_update_slice.30 = f32[4,512,1,256]{1,0,3,2:T(4,128)} dynamic-update-slice(f32[4,512,1,256]{1,0,3,2:T(4,128)} %get-tuple-element.387, f32[1,512,1,256]{1,0,3,2:T(1,128)S(1)} %copy.93, s32[]{:T(128)} %get-tuple-element.385, s32[]{:T(128)} %constant.83.clone.1..sunk, s32[]{:T(128)} %constant.83.clone.1..sunk, s32[]{:T(128)} %constant.83.clone.1..sunk) | dynamic-update-slice | bytes 1048580 | tf_op jit(solution)/shard_map/while/body/jit(dynamic_update_index_in_dim)/dynamic_update_slice | solution.py:191
  437.8 11.1 %dynamic_update_slice.29 = f32[4,512,1,256]{1,0,3,2:T(4,128)} dynamic-update-slice(f32[4,512,1,256]{1,0,3,2:T(4,128)} %get-tuple-element.386, f32[1,512,1,256]{1,0,3,2:T(1,128)S(1)} %copy.92, s32[]{:T(128)} %get-tuple-element.385, s32[]{:T(128)} %constant.83.clone.1..sunk, s32[]{:T(128)} %constant.83.clone.1..sunk, s32[]{:T(128)} %constant.83.clone.1..sunk) | dynamic-update-slice | bytes 1048580 | tf_op jit(solution)/shard_map/while/body/jit(dynamic_update_index_in_dim)/dynamic_update_slice | solution.py:191
  456.4 11.0 %dynamic_update_slice.30 = f32[4,512,1,256]{1,0,3,2:T(4,128)} dynamic-update-slice(f32[4,512,1,256]{1,0,3,2:T(4,128)} %get-tuple-element.387, f32[1,512,1,256]{1,0,3,2:T(1,128)S(1)} %copy.93, s32[]{:T(128)} %get-tuple-element.385, s32[]{:T(128)} %constant.83.clone.1..sunk, s32[]{:T(128)} %constant.83.clone.1..sunk, s32[]{:T(128)} %constant.83.clone.1..sunk) | dynamic-update-slice | bytes 1048580 | tf_op jit(solution)/shard_map/while/body/jit(dynamic_update_index_in_dim)/dynamic_update_slice | solution.py:191
  469.2 11.1 %dynamic_update_slice.29 = f32[4,512,1,256]{1,0,3,2:T(4,128)} dynamic-update-slice(f32[4,512,1,256]{1,0,3,2:T(4,128)} %get-tuple-element.386, f32[1,512,1,256]{1,0,3,2:T(1,128)S(1)} %copy.92, s32[]{:T(128)} %get-tuple-element.385, s32[]{:T(128)} %constant.83.clone.1..sunk, s32[]{:T(128)} %constant.83.clone.1..sunk, s32[]{:T(128)} %constant.83.clone.1..sunk) | dynamic-update-slice | bytes 1048580 | tf_op jit(solution)/shard_map/while/body/jit(dynamic_update_index_in_dim)/dynamic_update_slice | solution.py:191
  481.5 2.7 reshape.588
  484.2 3.7 reshape.591
  487.9 7.3 fusion.104
  502.2 2.5 add_convert_fusion
  506.5 4.3 fusion.124
  510.8 2.6 fusion.125
  517.0 4.1 fusion.123
  522.9 40.3 %all-reduce.4 = (f32[256]{0:T(256)}, f32[256]{0:T(256)}) all-reduce(f32[256]{0:T(256)S(1)} %get-tuple-element.156, f32[256]{0:T(256)S(1)} %get-tuple-element.154), channel_id=1, replica_groups=mesh['dp'=8,'tensor'=4] {'dp','tensor'}, use_global_device_ids=true, to_apply=%region_33.34 | all-reduce | flops 512 | bytes 4096 | tf_op jit(solution)/shard_map/psum | solution.py:314
  563.1 3.0 all-reduce.21.cloned.1.call-done
  566.2 4.0 fusion.56
  570.2 37.7 %all-reduce.6 = (f32[640]{0:T(1024)}, f32[640]{0:T(1024)}, f32[640]{0:T(1024)}, f32[640]{0:T(1024)}) all-reduce(f32[640]{0:T(1024)S(1)} %get-tuple-element.152, f32[640]{0:T(1024)S(1)} %get-tuple-element.146, f32[640]{0:T(1024)S(1)} %get-tuple-element.148, f32[640]{0:T(1024)S(1)} %get-tuple-element.150), channel_id=1, replica_groups=mesh['dp'=8,'tensor'=4] {'dp'}, use_global_device_ids=true, to_apply=%region_31.32 | all-reduce | flops 2560 | bytes 20480 | tf_op jit(solution)/shard_map/psum | solution.py:327
  607.9 5.5 fusion.60
  613.4 90.6 %all-reduce.23.cloned.1.call-done = (f32[640,256]{1,0:T(8,128)}, f32[640,256]{1,0:T(8,128)}) async-done(((f32[640,256]{1,0:T(8,128)}, f32[640,256]{1,0:T(8,128)}), (f32[640,256]{1,0:T(8,128)}, f32[640,256]{1,0:T(8,128)})) %all-reduce.23.cloned.1.call-update) | async-done | bytes 1310736 | tf_op jit(solution)/shard_map/psum | solution.py:314
  704.0 189.8 %all-reduce.25.cloned.1.call-done = (f32[640,256]{1,0:T(8,128)}, f32[256,640]{1,0:T(8,128)}, f32[640,512]{1,0:T(8,128)}, f32[640,512]{1,0:T(8,128)}, f32[512,640]{1,0:T(8,128)}) async-done(((f32[640,256]{1,0:T(8,128)}, f32[256,640]{1,0:T(8,128)}, f32[640,512]{1,0:T(8,128)}, f32[640,512]{1,0:T(8,128)}, f32[512,640]{1,0:T(8,128)}), (f32[640,256]{1,0:T(8,128)}, f32[256,640]{1,0:T(8,128)}, ...) | async-done | bytes 5242896 | tf_op jit(solution)/shard_map/psum | solution.py:327
  (296 shorter events, 112.7 us)
Async XLA Ops:
  7.2 188.3 %copy-start = (bf16[512,640]{1,0:T(8,128)(2,1)S(1)}, bf16[512,640]{1,0:T(8,128)(2,1)}, u32[]{:S(2)}) copy-start(bf16[512,640]{1,0:T(8,128)(2,1)} %param.28) | copy-start | bytes 1966084
  7.2 2.6 copy-start.4
  7.2 2.6 copy-start.62
  7.2 173.1 %all-reduce.15.cloned.1.call-start = ((), (), s32[]{:S(2)}) async-start(), calls=%async_computation | async-start | bytes 10485760 | tf_op jit(solution)/shard_map/psum | solution.py:263
  7.3 14.0 %copy-start.66 = (f32[128]{0:T(128)}, f32[128]{0:T(128)S(1)}, u32[]{:S(2)}) copy-start(f32[128]{0:T(128)S(1)} %multiply_power_fusion) | copy-start | bytes 1540
  10.8 4.7 copy-start.15
  13.2 5.4 copy-start.46
  15.5 5.8 copy-start.54
  15.5 3.0 copy-start.68
  15.5 3.0 copy-start.69
  15.5 3.0 copy-start.60
  15.6 5.7 copy-start.44
  18.6 2.7 copy-start.56
  18.6 2.7 copy-start.58
  18.6 2.7 copy-start.48
  35.6 3.7 copy-start.61
  74.9 184.1 %all-reduce.17.cloned.1.call-start = ((), (), s32[]{:S(2)}) async-start(), calls=%async_computation.1 | async-start | bytes 5242880 | tf_op jit(solution)/shard_map/psum | solution.py:266
  180.3 4.0 copy-start.2
  190.1 4.1 copy-start.70
  198.8 139.5 %all-reduce.19.cloned.1.call-start = ((), (), s32[]{:S(2)}) async-start(), calls=%async_computation.2 | async-start | bytes 5242880 | tf_op jit(solution)/shard_map/psum | solution.py:269
  261.5 4.2 copy-start.12
  261.5 5.7 copy-start.73
  267.2 5.6 copy-start.27
  267.9 4.9 copy-start.37
  278.1 288.0 %all-reduce.21.cloned.1.call-start = ((), (), s32[]{:S(2)}) async-start(), calls=%async_computation.3 | async-start | bytes 5242880 | tf_op jit(solution)/shard_map/psum | solution.py:272
  338.3 4.4 copy-start.13
  338.3 4.8 copy-start.18
  342.7 8.2 slice-start
  343.1 7.8 slice-start.1
  484.2 3.7 copy-start.49
  484.2 3.7 copy-start.67
  487.9 7.4 copy-start.8
  487.9 7.4 copy-start.47
  487.9 7.4 copy-start.59
  504.8 199.2 %all-reduce.23.cloned.1.call-start = ((), (), s32[]{:S(2)}) async-start(), calls=%async_computation.4 | async-start | bytes 2621440 | tf_op jit(solution)/shard_map/psum | solution.py:314
  506.5 4.3 copy-start.20
  510.8 2.6 copy-start.16
  510.8 2.6 copy-start.24
  516.9 4.1 copy-start.17
  517.0 376.8 %all-reduce.25.cloned.1.call-start = ((), (), s32[]{:S(2)}) async-start(), calls=%async_computation.5 | async-start | bytes 10485760 | tf_op jit(solution)/shard_map/psum | solution.py:327
  517.0 4.1 copy-start.22
  522.8 43.3 %copy-start.5 = (bf16[2048,640]{1,0:T(8,128)(2,1)S(1)}, bf16[2048,640]{1,0:T(8,128)(2,1)}, u32[]{:S(2)}) copy-start(bf16[2048,640]{1,0:T(8,128)(2,1)} %param.21) | copy-start | bytes 7864324
  563.1 44.7 %copy-start.51 = (f32[2048]{0:T(1024)S(1)}, f32[2048]{0:T(1024)}, u32[]{:S(2)}) copy-start(f32[2048]{0:T(1024)} %copy-done.50) | copy-start | bytes 24580
  704.0 193.9 %copy-start.34 = (f32[640,256]{1,0:T(8,128)S(1)}, f32[640,256]{1,0:T(8,128)}, u32[]{:S(2)}) copy-start(f32[640,256]{1,0:T(8,128)} %get-tuple-element.413) | copy-start | bytes 1966084
  893.8 4.9 copy-start.35
  893.8 5.8 copy-start.33
  897.9 2.7 copy-start.32
  899.6 3.2 copy-start.1
  (34 other events, 55.9 us)
Sparse Core Ops, SparseCore 0:
  75.0 105.2 all-reduce.14
  198.9 60.0 all-reduce.16
  278.3 59.9 all-reduce.18
  504.9 61.2 all-reduce.20
  572.2 131.7 all-reduce.22
  709.3 184.4 all-reduce.24
where the time goes:
time: 920 us; the launch traced here: 910 us
  waiting for transfers between devices  502 us (55%)
  local copies, waits for them, and re-layouts  153 us (17%)
  matrix products  95.9 us (10%)
  blocking collectives  77.9 us (8%)
  other arithmetic  63.7 us (7%)
  between operations  15.2 us (2%)
    psum x1, waiting for transfers between devices, on_device(): lax.psum((grad_query_weight, grad_output_weight, grad_gate_weight, grad_u...  190 us
    psum x1, waiting for transfers between devices, attention_reduce(): return lax.psum(values, 'tensor')  105 us
    dynamic_update_slice x16, local copies, waits for them, and re-layouts, run_layer(): lax.map(attend_back, (query_packs, key_packs, value_packs, segment_packs,...  92.6 us
    psum x1, waiting for transfers between devices, on_device(): lax.psum((grad_key_weight, grad_value_weight, grad_query_norm, grad_key_n...  90.6 us
    psum x1, waiting for transfers between devices, feed_reduce(): return lax.psum(values.astype(jnp.bfloat16), 'tensor').astype(jnp.float32)  59.6 us
    psum x1, waiting for transfers between devices, feed_back_reduce(): return lax.psum(values.astype(jnp.bfloat16), 'tensor').astype(jnp.float32)  54.6 us
    psum x1, blocking collectives, on_device(): lax.psum((grad_key_weight, grad_value_weight, grad_query_norm, grad_key_n...  40.3 us
    psum x1, blocking collectives, on_device(): lax.psum((grad_query_weight, grad_output_weight, grad_gate_weight, grad_u...  37.7 us
  transfers between devices with their start and end apart: 6, of which 6 were waited for; matrix products, arithmetic and copies ran while one was open for 3% of the time, Pallas kernels for 0%

commit v1 on v0

--- a/solution.py
+++ b/solution.py
@@ -7,6 +7,10 @@
 epsilon = 1e-06
 rope_base = 1000000.0
 masked_score = -1e30
+
+
+def unite_the_layers_all(v0):
+    return lax.all_gather(v0, axis_name="tensor").sum(axis=0)
 
 
 def normed(values, norm_gain):
@@ -260,7 +264,7 @@
 ):
 
     def attention_reduce(values):
-        return lax.psum(values, "tensor")
+        return unite_the_layers_all(values)
 
     def feed_reduce(values):
         return lax.psum(values.astype(jnp.bfloat16), "tensor").astype(jnp.float32)

time: 920 us -> 961 us (1.045)
  waiting for transfers between devices: 502 us -> 531 us
  other arithmetic: 63.7 us -> 74.4 us
    all_gather x0 -> x1, waiting for transfers between devices: none -> 134 us  [unite_the_layers_all(): return lax.all_gather(v0, axis_name='tensor').sum(axis=0)]
    psum x1 -> x0, waiting for transfers between devices: 105 us -> none  [attention_reduce(): return lax.psum(values, 'tensor')]
    reduce_sum x0 -> x1, other arithmetic: none -> 10.6 us  [unite_the_layers_all(): return lax.all_gather(v0, axis_name='tensor').sum(axis=0)]
where the time goes in v1:
time: 961 us; the launch traced here: 950 us
  waiting for transfers between devices  531 us (55%)
  local copies, waits for them, and re-layouts  154 us (16%)
  matrix products  95.8 us (10%)
  blocking collectives  78 us (8%)
  other arithmetic  74.4 us (8%)
  between operations  15.4 us (2%)
    psum x1, waiting for transfers between devices, on_device(): lax.psum((grad_query_weight, grad_output_weight, grad_gate_weight, grad_u...  190 us
    all_gather x1, waiting for transfers between devices, unite_the_layers_all(): return lax.all_gather(v0, axis_name='tensor').sum(axis=0)  134 us
    dynamic_update_slice x16, local copies, waits for them, and re-layouts, run_layer(): lax.map(attend_back, (query_packs, key_packs, value_packs, segment_packs,...  92.6 us
    psum x1, waiting for transfers between devices, on_device(): lax.psum((grad_key_weight, grad_value_weight, grad_query_norm, grad_key_n...  90.6 us
    psum x1, waiting for transfers between devices, feed_reduce(): return lax.psum(values.astype(jnp.bfloat16), 'tensor').astype(jnp.float32)  59.4 us
    psum x1, waiting for transfers between devices, feed_back_reduce(): return lax.psum(values.astype(jnp.bfloat16), 'tensor').astype(jnp.float32)  54.6 us
    psum x1, blocking collectives, on_device(): lax.psum((grad_key_weight, grad_value_weight, grad_query_norm, grad_key_n...  40.3 us
    psum x1, blocking collectives, on_device(): lax.psum((grad_query_weight, grad_output_weight, grad_gate_weight, grad_u...  37.7 us
  transfers between devices with their start and end apart: 6, of which 6 were waited for; matrix products, arithmetic and copies ran while one was open for 3% of the time, Pallas kernels for 0%

profile of v1, /device:TPU:0, one launch (start us, length us, event | category | flops | bytes accessed | tf_op | source)
XLA Modules:
  0.0 950.1 jit_solution(7494046543512947230)
XLA Ops:
  7.3 2.5 fusion.63
  11.4 2.3 multiply_reduce_fusion.6
  13.7 2.3 multiply_reduce_fusion.5
  16.1 3.0 copy.42
  19.2 2.7 multiply_bitcast_fusion
  21.8 5.7 fusion.99
  31.6 2.3 pad_maximum_fusion
  36.1 3.7 convolution_convert_fusion.4
  40.5 2.3 pad_maximum_fusion.1
  43.8 26.8 %while.26 = (s32[]{:T(128)}, bf16[4,512,1,256]{3,1,0,2:T(8,128)(2,1)}, f32[4,1,512,1]{2,3,1,0:T(1,128)}, bf16[4,512,256]{2,1,0:T(8,128)(2,1)}, s32[4,512]{1,0:T(...) while((s32[]{:T(128)}, bf16[4,512,1,256]{3,1,0,2:T(8,128)(2,1)}, ...), condition=%wide.region_6.7_spmd, body=%wide.region_3.6_spmd.sunk | while | flops 271187456 | bytes 5272153 | solution.py:138
  70.6 4.6 fusion.115
  76.0 133.8 %all-gather.3.cloned.1.call-done = f32[8192,640]{1,0:T(8,128)} async-done(((f32[2048,640]{1,0:T(8,128)}), f32[8192,640]{1,0:T(8,128)}) %all-gather.3.cloned.1.call-update) | async-done | bytes 20971536 | tf_op jit(solution)/shard_map/all_gather | solution.py:13
  209.8 10.6 %reduce_sum.198 = f32[2048,640]{1,0:T(8,128)} reduce(f32[4,2048,640]{2,1,0:T(8,128)} %bitcast.231, f32[]{:T(128)} %constant.85.clone.1), dimensions={0}, to_apply=%region_7.8 | reduce | flops 3932160 | bytes 26214404 | tf_op jit(solution)/shard_map/reduce_sum | solution.py:13
  220.4 3.0 multiply_reduce_fusion.4
  230.1 4.1 multiply_convert_fusion.3
  235.5 3.3 convolution_convert_fusion.2
  239.5 59.4 %all-reduce.14.cloned.1.call-done = bf16[2048,640]{1,0:T(8,128)(2,1)} async-done(((bf16[2048,640]{1,0:T(8,128)(2,1)}), bf16[2048,640]{1,0:T(8,128)(2,1)}) %all-reduce.14.cloned.1.call-update) | async-done | bytes 2621456 | tf_op jit(solution)/shard_map/psum | solution.py:270
  298.9 2.5 fusion.61
  301.4 4.2 fusion.57
  307.8 4.9 multiply_convert_fusion.2
  314.8 3.3 add_convert_fusion.1
  318.5 5.3 fusion.126
  323.7 54.6 %all-reduce.16.cloned.1.call-done = bf16[2048,640]{1,0:T(8,128)(2,1)} async-done(((bf16[2048,640]{1,0:T(8,128)(2,1)}), bf16[2048,640]{1,0:T(8,128)(2,1)}) %all-reduce.16.cloned.1.call-update) | async-done | bytes 2621456 | tf_op jit(solution)/shard_map/psum | solution.py:273
  378.4 4.4 fusion.55
  383.2 7.7 multiply_reduce_fusion.1
  395.9 125.7 %while.27 = (s32[]{:T(128)}, f32[4,512,1,256]{1,0,3,2:T(4,128)}, f32[4,512,1,256]{1,0,3,2:T(4,128)}, bf16[4,512,1,256]{3,1,0,2:T(8,128)(2,1)}, bf16[4,512,256]{2...) while((s32[]{:T(128)}, f32[4,512,1,256]{1,0,3,2:T(4,128)}, ...), condition=%wide.region_18.19_spmd, body=%wide.region_16.18_spmd.sunk | while | flops 674627072 | bytes 16275081 | solution.py:195
  402.1 11.0 %dynamic_update_slice.30 = f32[4,512,1,256]{1,0,3,2:T(4,128)} dynamic-update-slice(f32[4,512,1,256]{1,0,3,2:T(4,128)} %get-tuple-element.385, f32[1,512,1,256]{1,0,3,2:T(1,128)S(1)} %copy.94, s32[]{:T(128)} %get-tuple-element.383, s32[]{:T(128)} %constant.83.clone.1..sunk, s32[]{:T(128)} %constant.83.clone.1..sunk, s32[]{:T(128)} %constant.83.clone.1..sunk) | dynamic-update-slice | bytes 1048580 | tf_op jit(solution)/shard_map/while/body/jit(dynamic_update_index_in_dim)/dynamic_update_slice | solution.py:195
  415.0 11.0 %dynamic_update_slice.29 = f32[4,512,1,256]{1,0,3,2:T(4,128)} dynamic-update-slice(f32[4,512,1,256]{1,0,3,2:T(4,128)} %get-tuple-element.384, f32[1,512,1,256]{1,0,3,2:T(1,128)S(1)} %copy.93, s32[]{:T(128)} %get-tuple-element.383, s32[]{:T(128)} %constant.83.clone.1..sunk, s32[]{:T(128)} %constant.83.clone.1..sunk, s32[]{:T(128)} %constant.83.clone.1..sunk) | dynamic-update-slice | bytes 1048580 | tf_op jit(solution)/shard_map/while/body/jit(dynamic_update_index_in_dim)/dynamic_update_slice | solution.py:195
  433.6 11.0 %dynamic_update_slice.30 = f32[4,512,1,256]{1,0,3,2:T(4,128)} dynamic-update-slice(f32[4,512,1,256]{1,0,3,2:T(4,128)} %get-tuple-element.385, f32[1,512,1,256]{1,0,3,2:T(1,128)S(1)} %copy.94, s32[]{:T(128)} %get-tuple-element.383, s32[]{:T(128)} %constant.83.clone.1..sunk, s32[]{:T(128)} %constant.83.clone.1..sunk, s32[]{:T(128)} %constant.83.clone.1..sunk) | dynamic-update-slice | bytes 1048580 | tf_op jit(solution)/shard_map/while/body/jit(dynamic_update_index_in_dim)/dynamic_update_slice | solution.py:195
  446.4 11.0 %dynamic_update_slice.29 = f32[4,512,1,256]{1,0,3,2:T(4,128)} dynamic-update-slice(f32[4,512,1,256]{1,0,3,2:T(4,128)} %get-tuple-element.384, f32[1,512,1,256]{1,0,3,2:T(1,128)S(1)} %copy.93, s32[]{:T(128)} %get-tuple-element.383, s32[]{:T(128)} %constant.83.clone.1..sunk, s32[]{:T(128)} %constant.83.clone.1..sunk, s32[]{:T(128)} %constant.83.clone.1..sunk) | dynamic-update-slice | bytes 1048580 | tf_op jit(solution)/shard_map/while/body/jit(dynamic_update_index_in_dim)/dynamic_update_slice | solution.py:195
  465.0 11.0 %dynamic_update_slice.30 = f32[4,512,1,256]{1,0,3,2:T(4,128)} dynamic-update-slice(f32[4,512,1,256]{1,0,3,2:T(4,128)} %get-tuple-element.385, f32[1,512,1,256]{1,0,3,2:T(1,128)S(1)} %copy.94, s32[]{:T(128)} %get-tuple-element.383, s32[]{:T(128)} %constant.83.clone.1..sunk, s32[]{:T(128)} %constant.83.clone.1..sunk, s32[]{:T(128)} %constant.83.clone.1..sunk) | dynamic-update-slice | bytes 1048580 | tf_op jit(solution)/shard_map/while/body/jit(dynamic_update_index_in_dim)/dynamic_update_slice | solution.py:195
  477.8 11.0 %dynamic_update_slice.29 = f32[4,512,1,256]{1,0,3,2:T(4,128)} dynamic-update-slice(f32[4,512,1,256]{1,0,3,2:T(4,128)} %get-tuple-element.384, f32[1,512,1,256]{1,0,3,2:T(1,128)S(1)} %copy.93, s32[]{:T(128)} %get-tuple-element.383, s32[]{:T(128)} %constant.83.clone.1..sunk, s32[]{:T(128)} %constant.83.clone.1..sunk, s32[]{:T(128)} %constant.83.clone.1..sunk) | dynamic-update-slice | bytes 1048580 | tf_op jit(solution)/shard_map/while/body/jit(dynamic_update_index_in_dim)/dynamic_update_slice | solution.py:195
  496.4 11.0 %dynamic_update_slice.30 = f32[4,512,1,256]{1,0,3,2:T(4,128)} dynamic-update-slice(f32[4,512,1,256]{1,0,3,2:T(4,128)} %get-tuple-element.385, f32[1,512,1,256]{1,0,3,2:T(1,128)S(1)} %copy.94, s32[]{:T(128)} %get-tuple-element.383, s32[]{:T(128)} %constant.83.clone.1..sunk, s32[]{:T(128)} %constant.83.clone.1..sunk, s32[]{:T(128)} %constant.83.clone.1..sunk) | dynamic-update-slice | bytes 1048580 | tf_op jit(solution)/shard_map/while/body/jit(dynamic_update_index_in_dim)/dynamic_update_slice | solution.py:195
  509.3 11.0 %dynamic_update_slice.29 = f32[4,512,1,256]{1,0,3,2:T(4,128)} dynamic-update-slice(f32[4,512,1,256]{1,0,3,2:T(4,128)} %get-tuple-element.384, f32[1,512,1,256]{1,0,3,2:T(1,128)S(1)} %copy.93, s32[]{:T(128)} %get-tuple-element.383, s32[]{:T(128)} %constant.83.clone.1..sunk, s32[]{:T(128)} %constant.83.clone.1..sunk, s32[]{:T(128)} %constant.83.clone.1..sunk) | dynamic-update-slice | bytes 1048580 | tf_op jit(solution)/shard_map/while/body/jit(dynamic_update_index_in_dim)/dynamic_update_slice | solution.py:195
  521.6 2.7 reshape.588
  524.3 3.7 reshape.591
  528.0 7.4 fusion.104
  542.3 2.5 add_convert_fusion
  546.5 4.3 fusion.124
  550.9 2.6 fusion.125
  557.1 4.1 fusion.123
  562.9 40.3 %all-reduce.4 = (f32[256]{0:T(256)}, f32[256]{0:T(256)}) all-reduce(f32[256]{0:T(256)S(1)} %get-tuple-element.156, f32[256]{0:T(256)S(1)} %get-tuple-element.154), channel_id=1, replica_groups=mesh['dp'=8,'tensor'=4] {'dp','tensor'}, use_global_device_ids=true, to_apply=%region_33.34 | all-reduce | flops 512 | bytes 4096 | tf_op jit(solution)/shard_map/psum | solution.py:318
  603.2 3.0 all-reduce.18.cloned.1.call-done
  606.2 4.0 fusion.56
  610.2 37.7 %all-reduce.6 = (f32[640]{0:T(1024)}, f32[640]{0:T(1024)}, f32[640]{0:T(1024)}, f32[640]{0:T(1024)}) all-reduce(f32[640]{0:T(1024)S(1)} %get-tuple-element.152, f32[640]{0:T(1024)S(1)} %get-tuple-element.146, f32[640]{0:T(1024)S(1)} %get-tuple-element.148, f32[640]{0:T(1024)S(1)} %get-tuple-element.150), channel_id=1, replica_groups=mesh['dp'=8,'tensor'=4] {'dp'}, use_global_device_ids=true, to_apply=%region_31.32 | all-reduce | flops 2560 | bytes 20480 | tf_op jit(solution)/shard_map/psum | solution.py:331
  647.9 5.5 fusion.60
  653.4 90.6 %all-reduce.20.cloned.1.call-done = (f32[640,256]{1,0:T(8,128)}, f32[640,256]{1,0:T(8,128)}) async-done(((f32[640,256]{1,0:T(8,128)}, f32[640,256]{1,0:T(8,128)}), (f32[640,256]{1,0:T(8,128)}, f32[640,256]{1,0:T(8,128)})) %all-reduce.20.cloned.1.call-update) | async-done | bytes 1310736 | tf_op jit(solution)/shard_map/psum | solution.py:318
  744.0 189.8 %all-reduce.22.cloned.1.call-done = (f32[640,256]{1,0:T(8,128)}, f32[256,640]{1,0:T(8,128)}, f32[640,512]{1,0:T(8,128)}, f32[640,512]{1,0:T(8,128)}, f32[512,640]{1,0:T(8,128)}) async-done(((f32[640,256]{1,0:T(8,128)}, f32[256,640]{1,0:T(8,128)}, f32[640,512]{1,0:T(8,128)}, f32[640,512]{1,0:T(8,128)}, f32[512,640]{1,0:T(8,128)}), (f32[640,256]{1,0:T(8,128)}, f32[256,640]{1,0:T(8,128)}, ...) | async-done | bytes 5242896 | tf_op jit(solution)/shard_map/psum | solution.py:331
  (298 shorter events, 115.6 us)
Async XLA Ops:
  7.2 228.3 %copy-start = (bf16[512,640]{1,0:T(8,128)(2,1)S(1)}, bf16[512,640]{1,0:T(8,128)(2,1)}, u32[]{:S(2)}) copy-start(bf16[512,640]{1,0:T(8,128)(2,1)} %param.28) | copy-start | bytes 1966084
  7.2 3.2 copy-start.4
  7.2 3.2 copy-start.62
  7.2 202.6 %all-gather.3.cloned.1.call-start = ((), (), s32[]{:S(2)}) async-start(), calls=%async_computation.3 | async-start | bytes 26214400 | tf_op jit(solution)/shard_map/all_gather | solution.py:13
  7.3 14.5 %copy-start.66 = (f32[128]{0:T(128)}, f32[128]{0:T(128)S(1)}, u32[]{:S(2)}) copy-start(f32[128]{0:T(128)S(1)} %multiply_power_fusion) | copy-start | bytes 1540
  11.4 4.7 copy-start.15
  13.7 5.4 copy-start.46
  16.1 3.0 copy-start.56
  16.1 3.0 copy-start.68
  16.1 3.0 copy-start.69
  16.1 3.0 copy-start.60
  19.1 2.7 copy-start.58
  19.1 2.7 copy-start.48
  36.1 3.7 copy-start.61
  75.3 223.6 %all-reduce.14.cloned.1.call-start = ((), (), s32[]{:S(2)}) async-start(), calls=%async_computation | async-start | bytes 5242880 | tf_op jit(solution)/shard_map/psum | solution.py:270
  220.4 4.0 copy-start.2
  230.1 4.1 copy-start.70
  238.8 139.5 %all-reduce.16.cloned.1.call-start = ((), (), s32[]{:S(2)}) async-start(), calls=%async_computation.1 | async-start | bytes 5242880 | tf_op jit(solution)/shard_map/psum | solution.py:273
  301.4 4.2 copy-start.12
  301.4 5.7 copy-start.73
  307.1 5.6 copy-start.27
  307.8 4.9 copy-start.37
  318.2 288.0 %all-reduce.18.cloned.1.call-start = ((), (), s32[]{:S(2)}) async-start(), calls=%async_computation.2 | async-start | bytes 5242880 | tf_op jit(solution)/shard_map/psum | solution.py:276
  378.4 4.4 copy-start.13
  378.4 4.8 copy-start.18
  382.8 8.2 slice-start
  383.2 7.8 slice-start.1
  524.3 3.7 copy-start.49
  524.3 3.7 copy-start.67
  527.9 7.4 copy-start.8
  528.0 7.4 copy-start.47
  528.0 7.4 copy-start.59
  544.8 199.2 %all-reduce.20.cloned.1.call-start = ((), (), s32[]{:S(2)}) async-start(), calls=%async_computation.4 | async-start | bytes 2621440 | tf_op jit(solution)/shard_map/psum | solution.py:318
  546.5 4.3 copy-start.20
  550.9 2.6 copy-start.16
  550.9 2.6 copy-start.24
  557.0 4.1 copy-start.17
  557.0 376.8 %all-reduce.22.cloned.1.call-start = ((), (), s32[]{:S(2)}) async-start(), calls=%async_computation.5 | async-start | bytes 10485760 | tf_op jit(solution)/shard_map/psum | solution.py:331
  557.0 4.1 copy-start.22
  562.9 43.3 %copy-start.5 = (bf16[2048,640]{1,0:T(8,128)(2,1)S(1)}, bf16[2048,640]{1,0:T(8,128)(2,1)}, u32[]{:S(2)}) copy-start(bf16[2048,640]{1,0:T(8,128)(2,1)} %param.21) | copy-start | bytes 7864324
  562.9 43.3 %copy-start.45 = (f32[2048]{0:T(1024)S(1)}, f32[2048]{0:T(1024)}, u32[]{:S(2)}) copy-start(f32[2048]{0:T(1024)} %copy-done.44) | copy-start | bytes 24580
  562.9 43.3 %copy-start.55 = (f32[640]{0:T(1024)S(1)}, f32[640]{0:T(1024)}, u32[]{:S(2)}) copy-start(f32[640]{0:T(1024)} %copy-done.54) | copy-start | bytes 7684
  603.2 44.7 %copy-start.51 = (f32[2048]{0:T(1024)S(1)}, f32[2048]{0:T(1024)}, u32[]{:S(2)}) copy-start(f32[2048]{0:T(1024)} %copy-done.50) | copy-start | bytes 24580
  744.0 193.9 %copy-start.34 = (f32[640,256]{1,0:T(8,128)S(1)}, f32[640,256]{1,0:T(8,128)}, u32[]{:S(2)}) copy-start(f32[640,256]{1,0:T(8,128)} %get-tuple-element.411) | copy-start | bytes 1966084
  933.8 4.9 copy-start.35
  933.8 5.8 copy-start.33
  937.9 2.7 copy-start.32
  939.6 3.2 copy-start.1
  (34 other events, 53.4 us)
Sparse Core Ops, SparseCore 0:
  75.4 134.3 all-gather.2
  238.9 59.8 all-reduce.13
  318.3 60.0 all-reduce.15
  545.0 61.2 all-reduce.17
  612.2 131.7 all-reduce.19
  749.3 184.4 all-reduce.21
